TPU v7x, 256 devices: a whole 4x4x8 slice. The times are simulated.
256 devices in a mesh: member: 16 (over x_hi, z), space: 16 (over y, x_lo, core).
Axes of the slice: x: 4 (x_hi: 2, x_lo: 2; x = x_hi * 2 + x_lo), y: 4, z: 8, core: 2. Of those that a mesh axis runs over, the one named last changes fastest.
Arguments:
- alpha: float32 [32, 16, 128, 1280], P('member', None, 'space'), may hold values from -6 to 6
- perturb: bfloat16 [4, 32, 16, 128, 1280], P(None, 'member', None, 'space'), may hold values from -1 to 1
- kappa: float32 [128, 1280], P('space'), may hold values from 0.1 to 0.24
- land: int32 [128, 1280], P('space'), may hold values 0 or 1
- obs_weight: float32 [4, 16, 128, 1280], P(None, 'member', 'space'), may hold values from 0.2 to 5
- innovation: float32 [4, 16, 128, 1280], P(None, 'member', 'space'), may hold values from -6 to 6
Outputs:
- gradient: float32 [32, 16, 128, 1280], P('member', None, 'space')
- weighted_misfit: float32 [4, 16, 128, 1280], P(None, 'member', 'space')
All inputs are finite; a program needn't handle non-finite values. No bound on the sum of `land` on one device may be relied on, other than what follows from the above.
Results may differ from a plain program's by a relative error of at most 0.0003.
Values sent between devices are 32-bit elements; how exact they have to be, the bound alone decides.
A program may use at most 64 MiB of HBM per device.

v0:
```python
import jax
import jax.numpy as jnp
from jax import lax
from jax.sharding import PartitionSpec as P

STEPS = 4


def extended_2(cells, sides, width):
    for axis, dim in sides:
        count = lax.axis_size(axis)
        ends = count - 1
        head = lax.slice_in_dim(cells, 0, width, axis=dim)
        tail = lax.slice_in_dim(cells, cells.shape[dim] - width, cells.shape[dim], axis=dim)
        cells = jnp.concatenate(
            [
                lax.ppermute(tail, axis, [(i, (i + 1) % count) for i in range(ends)]),
                cells,
                lax.ppermute(head, axis, [((i + 1) % count, i) for i in range(ends)]),
            ],
            axis=dim,
        )
    return cells


def smooth_step(padded, coef_east, coef_west, coef_north, coef_south):
    middle = padded[:, :, 1:-1, :]
    return (
        middle
        + coef_east * (jnp.roll(middle, -1, axis=-1) - middle)
        + coef_west * (jnp.roll(middle, 1, axis=-1) - middle)
        + coef_north * (padded[:, :, 2:, :] - middle)
        + coef_south * (padded[:, :, :-2, :] - middle)
    )


def body(alpha, perturb, kappa, land, obs_weight, innovation):
    tile_rows = alpha.shape[2]
    extended = extended_2(kappa, (("space", 0),), STEPS + 1)
    inner = extended[1:-1]
    coef_north = 0.5 * (inner + extended[2:])
    coef_south = 0.5 * (inner + extended[:-2])
    coef_east = 0.5 * (inner + jnp.roll(inner, -1, axis=1))
    coef_west = 0.5 * (inner + jnp.roll(inner, 1, axis=1))

    def diffuse(field):
        current = field
        for sweep in range(STEPS):
            padded = extended_2(current, (("space", 2),), 1)
            current = smooth_step(
                padded,
                coef_east[STEPS : STEPS + tile_rows],
                coef_west[STEPS : STEPS + tile_rows],
                coef_north[STEPS : STEPS + tile_rows],
                coef_south[STEPS : STEPS + tile_rows],
            )
        return current

    sea = land.astype(jnp.float32)
    local = diffuse(alpha) * sea
    partial_sum = jnp.sum(perturb * local[None], axis=1)
    total = lax.psum(partial_sum, "member")
    weight_all, innov_all = (
        lax.all_gather(obs_weight, "member", axis=1, tiled=True),
        lax.all_gather(innovation, "member", axis=1, tiled=True),
    )
    whole_misfit = weight_all * (total - innov_all)
    own_width = obs_weight.shape[1]
    weighted_misfit = lax.dynamic_slice_in_dim(
        whole_misfit, lax.axis_index("member") * own_width, own_width, 1
    )
    back = jnp.sum(perturb * whole_misfit[:, None], axis=0)
    gradient = diffuse(back * sea) + alpha
    return (gradient, weighted_misfit)


def solution(mesh):
    placed = (
        P("member", None, "space", None),
        P(None, "member", None, "space", None),
        P("space", None),
        P("space", None),
        P(None, "member", "space", None),
        P(None, "member", "space", None),
    )
    return jax.shard_map(
        body,
        mesh=mesh,
        in_specs=placed,
        out_specs=(P("member", None, "space", None), P(None, "member", "space", None)),
        check_vma=False,
    )
```

profile of v0, /device:TPU:8, one launch (start us, length us, event | category | flops | bytes accessed | tf_op | source)
XLA Modules:
  0.0 468.6 jit_solution(17923202716752243440)
XLA Ops:
  7.2 0.9 fusion.116
  8.1 1.9 collective-permute-start
  10.0 4.5 collective-permute-start.1
  14.6 2.1 fusion.113
  16.7 1.9 collective-permute-start.2
  18.7 2.5 collective-permute-start.3
  21.2 0.4 fusion.112
  22.2 4.1 collective-permute-done.3
  26.5 1.0 fusion.48
  27.5 0.4 fusion.109
  28.0 0.2 fusion.110
  28.2 1.9 collective-permute-start.4
  30.1 2.4 collective-permute-start.5
  32.7 0.3 collective-permute-done.4
  33.1 4.6 collective-permute-done.5
  37.9 1.0 fusion.42
  38.9 0.4 fusion.106
  39.5 1.9 collective-permute-start.6
  41.5 2.4 collective-permute-start.7
  44.0 0.3 collective-permute-done.6
  44.5 4.6 collective-permute-done.7
  49.2 1.0 fusion.36
  50.2 0.4 fusion.103
  50.9 1.9 collective-permute-start.8
  52.8 2.4 collective-permute-start.9
  55.3 0.3 collective-permute-done.8
  55.8 4.6 collective-permute-done.9
  60.6 1.1 fusion.30
  61.6 0.7 copy-done.1
  62.3 2.1 fusion
  64.5 0.7 all-gather.3.cloned.1.call-update
  65.2 0.2 all-gather.5.cloned.1.call-start
  65.4 0.5 all-gather.5.cloned.1.call-update
  65.9 166.5 %all-reduce.2.cloned.1.call-done = f32[4,16,8,1280]{3,2,1,0:T(8,128)} async-done(((f32[4,16,8,1280]{3,2,1,0:T(8,128)}), f32[4,16,8,1280]{3,2,1,0:T(8,128)}) %all-reduce.2.cloned.1.call-update) | async-done | bytes 2621456 | tf_op jit(solution)/shard_map/psum | solution.py:62
  232.4 89.5 %all-gather.3.cloned.1.call-done = f32[4,16,8,1280]{3,2,1,0:T(8,128)} async-done(((f32[4,1,8,1280]{3,2,1,0:T(8,128)}), f32[4,16,8,1280]{3,2,1,0:T(8,128)}) %all-gather.3.cloned.1.call-update) | async-done | bytes 2621456 | tf_op jit(solution)/shard_map/all_gather | solution.py:64
  321.9 88.8 %all-gather.5.cloned.1.call-done = f32[4,16,8,1280]{3,2,1,0:T(8,128)} async-done(((f32[4,1,8,1280]{3,2,1,0:T(8,128)}), f32[4,16,8,1280]{3,2,1,0:T(8,128)}) %all-gather.5.cloned.1.call-update) | async-done | bytes 2621456 | tf_op jit(solution)/shard_map/all_gather | solution.py:65
  410.7 3.9 subtract_multiply_fusion
  414.8 0.6 fusion.1
  415.4 0.4 fusion.100
  415.9 0.2 fusion.101
  416.2 1.9 collective-permute-start.10
  418.1 2.4 collective-permute-start.11
  420.6 0.7 constant_dynamic-slice_fusion
  421.4 4.3 collective-permute-done.11
  425.9 1.0 fusion.23
  426.9 0.4 fusion.97
  427.5 1.9 collective-permute-start.12
  429.5 2.4 collective-permute-start.13
  432.0 0.3 collective-permute-done.12
  432.5 4.6 collective-permute-done.13
  437.2 1.0 fusion.17
  438.2 0.4 fusion.94
  438.6 0.2 fusion.95
  438.9 1.9 collective-permute-start.14
  440.8 2.4 collective-permute-start.15
  443.3 0.3 collective-permute-done.14
  443.8 4.6 collective-permute-done.15
  448.5 1.1 fusion.11
  449.6 0.4 fusion.91
  450.3 1.9 collective-permute-start.16
  452.2 2.4 collective-permute-start.17
  454.7 0.3 collective-permute-done.16
  455.2 4.6 collective-permute-done.17
  459.9 2.2 fusion.5
  (66 shorter events, 5.0 us)
Async XLA Ops:
  7.2 14.1 %copy-start = (f32[2,16,8,1280]{3,2,1,0:T(8,128)S(1)}, f32[2,16,8,1280]{3,2,1,0:T(8,128)}, u32[]{:S(2)}) copy-start(f32[2,16,8,1280]{3,2,1,0:T(8,128)} %param.6) | copy-start | bytes 3932164
  7.2 225.2 %all-reduce.2.cloned.1.call-start = ((), (), s32[]{:S(2)}) async-start(), calls=%async_computation.1 | async-start | bytes 5242880 | tf_op jit(solution)/shard_map/psum | solution.py:62
  8.1 13.7 %collective-permute-start = (f32[5,1280]{1,0:T(8,128)S(1)}, f32[5,1280]{1,0:T(8,128)S(1)}, u32[]{:S(2)}, u32[]{:S(2)}) collective-permute-start(f32[5,1280]{1,0:T(8,128)S(1)} %get-tuple-element.61), channel_id=1, source_target_pairs={{0,1},{1,2},{2,3},{3,4},{4,5},{5,6},{6,7},{7,8},{8,9},{9,10},{10,1... | collective-permute-start | bytes 76808 | tf_op jit(solution)/shard_map/ppermute | solution.py:17
  10.0 11.8 %collective-permute-start.1 = (f32[5,1280]{1,0:T(8,128)S(1)}, f32[5,1280]{1,0:T(8,128)S(1)}, u32[]{:S(2)}, u32[]{:S(2)}) collective-permute-start(f32[5,1280]{1,0:T(8,128)S(1)} %get-tuple-element.62), channel_id=1, source_target_pairs={{1,0},{2,1},{3,2},{4,3},{5,4},{6,5},{7,6},{8,7},{9,8},{10,9},{11,1... | collective-permute-start | bytes 76808 | tf_op jit(solution)/shard_map/ppermute | solution.py:19
  16.7 5.4 %collective-permute-start.2 = (f32[2,16,1,1280]{3,1,2,0:T(8,128)S(1)}, f32[2,16,1,1280]{3,1,2,0:T(8,128)S(1)}, u32[]{:S(2)}, u32[]{:S(2)}) collective-permute-start(f32[2,16,1,1280]{3,1,2,0:T(8,128)S(1)} %copy.56), channel_id=1, source_target_pairs={{1,0},{2,1},{3,2},{4,3},{5,4},{6,5},{7,6},{8,7},{9,8},{10,9},{11,1... | collective-permute-start | bytes 491528 | tf_op jit(solution)/shard_map/ppermute | solution.py:19
  18.6 3.1 copy-start.4
  18.7 3.1 copy-start.3
  18.7 7.7 %collective-permute-start.3 = (f32[2,16,1,1280]{3,1,2,0:T(8,128)S(1)}, f32[2,16,1,1280]{3,1,2,0:T(8,128)S(1)}, u32[]{:S(2)}, u32[]{:S(2)}) collective-permute-start(f32[2,16,1,1280]{3,1,2,0:T(8,128)S(1)} %copy.57), channel_id=1, source_target_pairs={{0,1},{1,2},{2,3},{3,4},{4,5},{5,6},{6,7},{7,8},{8,9},{9,10},{10,1... | collective-permute-start | bytes 491528 | tf_op jit(solution)/shard_map/ppermute | solution.py:17
  28.2 4.7 %collective-permute-start.4 = (f32[2,16,1,1280]{3,1,2,0:T(8,128)S(1)}, f32[2,16,1,1280]{3,1,2,0:T(8,128)S(1)}, u32[]{:S(2)}, u32[]{:S(2)}) collective-permute-start(f32[2,16,1,1280]{3,1,2,0:T(8,128)S(1)} %copy.28), channel_id=1, source_target_pairs={{1,0},{2,1},{3,2},{4,3},{5,4},{6,5},{7,6},{8,7},{9,8},{10,9},{11,1... | collective-permute-start | bytes 491528 | tf_op jit(solution)/shard_map/ppermute | solution.py:19
  30.1 7.5 %collective-permute-start.5 = (f32[2,16,1,1280]{3,1,2,0:T(8,128)S(1)}, f32[2,16,1,1280]{3,1,2,0:T(8,128)S(1)}, u32[]{:S(2)}, u32[]{:S(2)}) collective-permute-start(f32[2,16,1,1280]{3,1,2,0:T(8,128)S(1)} %copy.30), channel_id=1, source_target_pairs={{0,1},{1,2},{2,3},{3,4},{4,5},{5,6},{6,7},{7,8},{8,9},{9,10},{10,1... | collective-permute-start | bytes 491528 | tf_op jit(solution)/shard_map/ppermute | solution.py:17
  39.5 4.7 %collective-permute-start.6 = (f32[2,16,1,1280]{3,1,2,0:T(8,128)S(1)}, f32[2,16,1,1280]{3,1,2,0:T(8,128)S(1)}, u32[]{:S(2)}, u32[]{:S(2)}) collective-permute-start(f32[2,16,1,1280]{3,1,2,0:T(8,128)S(1)} %copy.32), channel_id=1, source_target_pairs={{1,0},{2,1},{3,2},{4,3},{5,4},{6,5},{7,6},{8,7},{9,8},{10,9},{11,1... | collective-permute-start | bytes 491528 | tf_op jit(solution)/shard_map/ppermute | solution.py:19
  41.5 7.5 %collective-permute-start.7 = (f32[2,16,1,1280]{3,1,2,0:T(8,128)S(1)}, f32[2,16,1,1280]{3,1,2,0:T(8,128)S(1)}, u32[]{:S(2)}, u32[]{:S(2)}) collective-permute-start(f32[2,16,1,1280]{3,1,2,0:T(8,128)S(1)} %copy.34), channel_id=1, source_target_pairs={{0,1},{1,2},{2,3},{3,4},{4,5},{5,6},{6,7},{7,8},{8,9},{9,10},{10,1... | collective-permute-start | bytes 491528 | tf_op jit(solution)/shard_map/ppermute | solution.py:17
  50.9 4.7 %collective-permute-start.8 = (f32[2,16,1,1280]{3,1,2,0:T(8,128)S(1)}, f32[2,16,1,1280]{3,1,2,0:T(8,128)S(1)}, u32[]{:S(2)}, u32[]{:S(2)}) collective-permute-start(f32[2,16,1,1280]{3,1,2,0:T(8,128)S(1)} %copy.36), channel_id=1, source_target_pairs={{1,0},{2,1},{3,2},{4,3},{5,4},{6,5},{7,6},{8,7},{9,8},{10,9},{11,1... | collective-permute-start | bytes 491528 | tf_op jit(solution)/shard_map/ppermute | solution.py:19
  52.8 7.5 %collective-permute-start.9 = (f32[2,16,1,1280]{3,1,2,0:T(8,128)S(1)}, f32[2,16,1,1280]{3,1,2,0:T(8,128)S(1)}, u32[]{:S(2)}, u32[]{:S(2)}) collective-permute-start(f32[2,16,1,1280]{3,1,2,0:T(8,128)S(1)} %copy.38), channel_id=1, source_target_pairs={{0,1},{1,2},{2,3},{3,4},{4,5},{5,6},{6,7},{7,8},{8,9},{9,10},{10,1... | collective-permute-start | bytes 491528 | tf_op jit(solution)/shard_map/ppermute | solution.py:17
  60.5 1.7 copy-start.1
  64.5 257.5 %all-gather.3.cloned.1.call-start = ((), (), s32[]{:S(2)}) async-start(), calls=%async_computation | async-start | bytes 2785280 | tf_op jit(solution)/shard_map/all_gather | solution.py:64
  65.2 345.5 %all-gather.5.cloned.1.call-start = ((), (), s32[]{:S(2)}) async-start(), calls=%async_computation.2 | async-start | bytes 2785280 | tf_op jit(solution)/shard_map/all_gather | solution.py:65
  410.7 4.0 copy-start.2
  416.2 5.1 %collective-permute-start.10 = (f32[2,16,1,1280]{3,1,2,0:T(8,128)S(1)}, f32[2,16,1,1280]{3,1,2,0:T(8,128)S(1)}, u32[]{:S(2)}, u32[]{:S(2)}) collective-permute-start(f32[2,16,1,1280]{3,1,2,0:T(8,128)S(1)} %copy.40), channel_id=1, source_target_pairs={{1,0},{2,1},{3,2},{4,3},{5,4},{6,5},{7,6},{8,7},{9,8},{10,9},{11,1... | collective-permute-start | bytes 491528 | tf_op jit(solution)/shard_map/ppermute | solution.py:19
  418.1 7.5 %collective-permute-start.11 = (f32[2,16,1,1280]{3,1,2,0:T(8,128)S(1)}, f32[2,16,1,1280]{3,1,2,0:T(8,128)S(1)}, u32[]{:S(2)}, u32[]{:S(2)}) collective-permute-start(f32[2,16,1,1280]{3,1,2,0:T(8,128)S(1)} %copy.42), channel_id=1, source_target_pairs={{0,1},{1,2},{2,3},{3,4},{4,5},{5,6},{6,7},{7,8},{8,9},{9,10},{10,1... | collective-permute-start | bytes 491528 | tf_op jit(solution)/shard_map/ppermute | solution.py:17
  427.5 4.7 %collective-permute-start.12 = (f32[2,16,1,1280]{3,1,2,0:T(8,128)S(1)}, f32[2,16,1,1280]{3,1,2,0:T(8,128)S(1)}, u32[]{:S(2)}, u32[]{:S(2)}) collective-permute-start(f32[2,16,1,1280]{3,1,2,0:T(8,128)S(1)} %copy.44), channel_id=1, source_target_pairs={{1,0},{2,1},{3,2},{4,3},{5,4},{6,5},{7,6},{8,7},{9,8},{10,9},{11,1... | collective-permute-start | bytes 491528 | tf_op jit(solution)/shard_map/ppermute | solution.py:19
  429.5 7.5 %collective-permute-start.13 = (f32[2,16,1,1280]{3,1,2,0:T(8,128)S(1)}, f32[2,16,1,1280]{3,1,2,0:T(8,128)S(1)}, u32[]{:S(2)}, u32[]{:S(2)}) collective-permute-start(f32[2,16,1,1280]{3,1,2,0:T(8,128)S(1)} %copy.46), channel_id=1, source_target_pairs={{0,1},{1,2},{2,3},{3,4},{4,5},{5,6},{6,7},{7,8},{8,9},{9,10},{10,1... | collective-permute-start | bytes 491528 | tf_op jit(solution)/shard_map/ppermute | solution.py:17
  438.9 4.7 %collective-permute-start.14 = (f32[2,16,1,1280]{3,1,2,0:T(8,128)S(1)}, f32[2,16,1,1280]{3,1,2,0:T(8,128)S(1)}, u32[]{:S(2)}, u32[]{:S(2)}) collective-permute-start(f32[2,16,1,1280]{3,1,2,0:T(8,128)S(1)} %copy.48), channel_id=1, source_target_pairs={{1,0},{2,1},{3,2},{4,3},{5,4},{6,5},{7,6},{8,7},{9,8},{10,9},{11,1... | collective-permute-start | bytes 491528 | tf_op jit(solution)/shard_map/ppermute | solution.py:19
  440.8 7.5 %collective-permute-start.15 = (f32[2,16,1,1280]{3,1,2,0:T(8,128)S(1)}, f32[2,16,1,1280]{3,1,2,0:T(8,128)S(1)}, u32[]{:S(2)}, u32[]{:S(2)}) collective-permute-start(f32[2,16,1,1280]{3,1,2,0:T(8,128)S(1)} %copy.50), channel_id=1, source_target_pairs={{0,1},{1,2},{2,3},{3,4},{4,5},{5,6},{6,7},{7,8},{8,9},{9,10},{10,1... | collective-permute-start | bytes 491528 | tf_op jit(solution)/shard_map/ppermute | solution.py:17
  450.3 4.7 %collective-permute-start.16 = (f32[2,16,1,1280]{3,1,2,0:T(8,128)S(1)}, f32[2,16,1,1280]{3,1,2,0:T(8,128)S(1)}, u32[]{:S(2)}, u32[]{:S(2)}) collective-permute-start(f32[2,16,1,1280]{3,1,2,0:T(8,128)S(1)} %copy.52), channel_id=1, source_target_pairs={{1,0},{2,1},{3,2},{4,3},{5,4},{6,5},{7,6},{8,7},{9,8},{10,9},{11,1... | collective-permute-start | bytes 491528 | tf_op jit(solution)/shard_map/ppermute | solution.py:19
  452.2 7.5 %collective-permute-start.17 = (f32[2,16,1,1280]{3,1,2,0:T(8,128)S(1)}, f32[2,16,1,1280]{3,1,2,0:T(8,128)S(1)}, u32[]{:S(2)}, u32[]{:S(2)}) collective-permute-start(f32[2,16,1,1280]{3,1,2,0:T(8,128)S(1)} %copy.54), channel_id=1, source_target_pairs={{0,1},{1,2},{2,3},{3,4},{4,5},{5,6},{6,7},{7,8},{8,9},{9,10},{10,1... | collective-permute-start | bytes 491528 | tf_op jit(solution)/shard_map/ppermute | solution.py:17
Sparse Core Ops, SparseCore 0:
  64.6 167.7 all-reduce.1
  235.0 86.8 all-gather.2
  324.5 86.1 all-gather.4
where the time goes:
time: 469 us
  waiting for transfers between devices  383 us (82%)
  starting transfers between devices  41.5 us (9%)
  other arithmetic  16.3 us (3%)
  between operations  14.4 us (3%)
  local copies, waits for them, and re-layouts  13 us (3%)
    psum x1, waiting for transfers between devices, body(): total = lax.psum(partial_sum, 'member')  166 us
    all_gather x1, waiting for transfers between devices, body(): lax.all_gather(obs_weight, 'member', axis=1, tiled=True)  89.5 us
    all_gather x1, waiting for transfers between devices, body(): lax.all_gather(innovation, 'member', axis=1, tiled=True)  88.8 us
    ppermute x9, waiting for transfers between devices, extended_2(): lax.ppermute(tail, axis, [(i, (i + 1) % count) for i in range(ends)])  35.8 us
    ppermute x9, starting transfers between devices, extended_2(): lax.ppermute(tail, axis, [(i, (i + 1) % count) for i in range(ends)])  21.3 us
    ppermute x9, starting transfers between devices, extended_2(): lax.ppermute(head, axis, [((i + 1) % count, i) for i in range(ends)])  19.9 us
  transfers between devices with their start and end apart: 21, of which 17 were waited for; matrix products, arithmetic and copies ran while one was open for 1% of the time, Pallas kernels for 0%

commit v1 on v0

v1 whole, which is shorter than its diff:
```python
import jax
import jax.numpy as jnp
from jax import lax
from jax.experimental import pallas as pl
from jax.experimental.pallas import tpu as pltpu
from jax.sharding import PartitionSpec as P

STEPS = 4
ROWS = 8
LON = 1280
HALO = 4
RING = 8
PAIR = 2
SLOTS = 4
OWN = 2
SPACE = 16
MESH = pl.DeviceIdType.MESH
DOWN, UP = 0, 1
REACH = {DOWN: (4, 4, 3, 3), UP: (3, 3, 4, 4)}
NEAR_LAST = (4, -3, 3, -2, 2, -1, 1, 0)


def kernel(
    alpha, perturb, kappa, land, weight, innov,
    grad_out, misfit_out,
    al, pe, halo_f, halo_b, back, result, kap, coef, sea_i, sea,
    local, ring, total, across, obs, misfit,
    in_sem, out_sem, kap_sem, hf_send, hf_recv, hb_send, hb_recv,
    rs_send, rs_recv, x_send, x_recv, ob_send, ob_recv, ag_send, ag_recv,
):
    member = lax.axis_index("member")
    space = lax.axis_index("space")
    pair = member // RING
    depth = lax.rem(member, RING)
    below = (pair * RING + lax.rem(depth + RING - 1, RING), space)
    above = (pair * RING + lax.rem(depth + 1, RING), space)
    opposite = ((1 - pair) * RING + depth, space)
    north = (member, lax.rem(space + 1, SPACE))
    south = (member, lax.rem(space + SPACE - 1, SPACE))
    toward = {DOWN: below, UP: above}

    def at(off):
        return lax.rem(depth + (off + RING), RING)

    def remote(src, dst, send, recv, device):
        return pltpu.make_async_remote_copy(
            src_ref=src, dst_ref=dst, send_sem=send, recv_sem=recv, device_id=device, device_id_type=MESH
        )

    sent = []

    def go(copy):
        copy.start()
        sent.append(copy)

    loads = [
        pltpu.make_async_copy(kappa, kap.at[pl.ds(0, ROWS)], in_sem.at[0]),
        pltpu.make_async_copy(alpha, al, in_sem.at[1]),
        pltpu.make_async_copy(land, sea_i, in_sem.at[2]),
        pltpu.make_async_copy(perturb, pe, in_sem.at[3]),
        pltpu.make_async_copy(weight, obs.at[pair, 0], in_sem.at[4]),
        pltpu.make_async_copy(innov, obs.at[pair, 1], in_sem.at[5]),
    ]
    for load in loads:
        load.start()

    barrier = pltpu.get_barrier_semaphore()
    for device in (below, above, opposite, north, south):
        pl.semaphore_signal(barrier, inc=1, device_id=device, device_id_type=MESH)
    pl.semaphore_wait(barrier, 5)

    low, high = pl.ds(0, HALO), pl.ds(HALO, HALO)
    kap_copies = (
        remote(kappa.at[high], kap.at[pl.ds(ROWS + HALO, HALO)], kap_sem.at[0], kap_sem.at[1], north),
        remote(kappa.at[low], kap.at[pl.ds(ROWS, HALO)], kap_sem.at[2], kap_sem.at[3], south),
    )

    def edges(src, dst, send, recv, off):
        z = at(off)
        j = off % RING
        return (
            remote(src.at[:, :, z, high], dst.at[:, :, z, high], send.at[j, 0], recv.at[j, 0], north),
            remote(src.at[:, :, z, low], dst.at[:, :, z, low], send.at[j, 1], recv.at[j, 1], south),
        )

    forward = {off: edges(alpha, halo_f, hf_send, hf_recv, off) for off in NEAR_LAST}
    backward = {off: edges(back, halo_b, hb_send, hb_recv, off) for off in NEAR_LAST}
    observed = (
        remote(weight, obs.at[pair, 0], ob_send.at[0], ob_recv.at[0], opposite),
        remote(innov, obs.at[pair, 1], ob_send.at[1], ob_recv.at[1], opposite),
    )
    scatter = {
        (way, k, t): remote(
            ring.at[way, k, t], ring.at[way, k - 1, t],
            rs_send.at[way, k - 1, t], rs_recv.at[way, k - 1, t], toward[way],
        )
        for way in (DOWN, UP) for t in range(SLOTS) for k in range(1, REACH[way][t] + 1)
    }
    cross = [remote(total.at[t], across.at[t], x_send.at[t], x_recv.at[t], opposite) for t in range(SLOTS)]

    def gather_copy(way, k, t):
        z = at(k if way == DOWN else -k)
        return remote(
            misfit.at[z, t], misfit.at[z, t], ag_send.at[way, k, t], ag_recv.at[way, k, t], toward[way]
        )

    gather = {
        (way, k, t): gather_copy(way, k, t)
        for way in (DOWN, UP) for t in range(SLOTS) for k in range(REACH[way][t])
    }

    def send_edges(copies):
        for copy in copies:
            go(copy)

    send_edges(kap_copies)
    send_edges(forward[NEAR_LAST[0]])
    send_edges(forward[NEAR_LAST[1]])

    loads[0].wait()
    for copy in kap_copies:
        copy.wait_recv()
    row = lax.broadcasted_iota(jnp.int32, (2 * ROWS, LON), 0)
    inside = (row < ROWS) | ((row < ROWS + HALO) & (space < SPACE - 1)) | ((row >= ROWS + HALO) & (space > 0))
    k16 = jnp.where(inside, kap[...], 0.0)
    east = 0.5 * (k16 + pltpu.roll(k16, LON - 1, 1))
    west = 0.5 * (k16 + pltpu.roll(k16, 1, 1))
    up = 0.5 * (k16 + pltpu.roll(k16, 2 * ROWS - 1, 0))
    down = 0.5 * (k16 + pltpu.roll(k16, 1, 0))
    for i, c in enumerate((1.0 - (east + west + up + down), east, west, up, down)):
        coef[i] = jnp.where(inside, c, 0.0)
    loads[2].wait()
    sea[...] = sea_i[...].astype(jnp.float32)

    def smooth(tile, edge):
        row8 = lax.broadcasted_iota(jnp.int32, (ROWS, LON), 0)
        known = ((row8 < HALO) & (space < SPACE - 1)) | ((row8 >= HALO) & (space > 0))
        u = jnp.concatenate([tile, jnp.where(known, edge, 0.0)], axis=0)
        for step in range(STEPS):
            n = 2 * ROWS if step < STEPS - 1 else ROWS
            terms = (
                u,
                pltpu.roll(u, LON - 1, 1),
                pltpu.roll(u, 1, 1),
                pltpu.roll(u, 2 * ROWS - 1, 0),
                pltpu.roll(u, 1, 0),
            )
            acc = coef[0, :n] * terms[0][:n]
            for i in range(1, 5):
                acc = acc + coef[i, :n] * terms[i][:n]
            u = acc
        return u

    def diffuse_forward(off):
        for copy in forward[off]:
            copy.wait_recv()
        z = at(off)

        @pl.loop(0, OWN * PAIR)
        def _(i):
            m, p = i // PAIR, lax.rem(i, PAIR)
            local[m, p, z] = smooth(al[m, p, z], halo_f[m, p, z]) * sea[...]

    def partial(off, t, p):
        z = at(off)
        return (
            pe[t, 0, p, z].astype(jnp.float32) * local[0, p, z]
            + pe[t, 1, p, z].astype(jnp.float32) * local[1, p, z]
        )

    def scatter_step(way, k, t):
        off = -k if way == DOWN else k
        if k < REACH[way][t]:
            scatter[way, k + 1, t].wait_recv()
        for p in range(PAIR):
            part = partial(off, t, p)
            if k < REACH[way][t]:
                part = part + ring[way, k, t, p]
            ring[way, k, t, p] = part
        go(scatter[way, k, t])

    def cross_step(t):
        for way in (DOWN, UP):
            scatter[way, 1, t].wait_recv()
        for p in range(PAIR):
            total[t, p] = partial(0, t, p) + ring[DOWN, 0, t, p] + ring[UP, 0, t, p]
        go(cross[t])

    stored = []

    def misfit_step(t):
        cross[t].wait_recv()
        for p in range(PAIR):
            misfit[depth, t, p] = obs[p, 0, t] * (total[t, p] + across[t, p] - obs[p, 1, t])
        for way in (DOWN, UP):
            go(gather[way, 0, t])
        copy = pltpu.make_async_copy(misfit.at[depth, t, pair], misfit_out.at[t], out_sem.at[RING + t])
        copy.start()
        stored.append(copy)

    def relay(way, k, t):
        gather[way, k - 1, t].wait_recv()
        if k < REACH[way][t]:
            go(gather[way, k, t])

    def adjoint(off):
        z = at(off)

        @pl.loop(0, OWN * PAIR)
        def _(i):
            m, p = i // PAIR, lax.rem(i, PAIR)
            acc = pe[0, m, p, z].astype(jnp.float32) * misfit[z, 0, p]
            for t in range(1, SLOTS):
                acc = acc + pe[t, m, p, z].astype(jnp.float32) * misfit[z, t, p]
            back[m, p, z] = acc * sea[...]

        send_edges(backward[off])

    def diffuse_backward(off):
        for copy in backward[off]:
            copy.wait_recv()
        z = at(off)

        @pl.loop(0, OWN * PAIR)
        def _(i):
            m, p = i // PAIR, lax.rem(i, PAIR)
            result[m, p, z] = smooth(back[m, p, z], halo_b[m, p, z]) + al[m, p, z]

        copy = pltpu.make_async_copy(result.at[:, :, z], grad_out.at[:, :, z], out_sem.at[off % RING])
        copy.start()
        stored.append(copy)

    a, b, c, d = range(SLOTS)
    loads[1].wait()
    diffuse_forward(4)
    send_edges(forward[3])
    loads[3].wait()
    for way, t in ((DOWN, a), (UP, c), (DOWN, b), (UP, d)):
        scatter_step(way, 4, t)
    diffuse_forward(-3)
    send_edges(forward[-2])
    for t in (c, d):
        scatter_step(DOWN, 3, t)
    diffuse_forward(3)
    send_edges(forward[2])
    for t in (a, b):
        scatter_step(UP, 3, t)
    for t1, t2 in ((a, c), (b, d)):
        scatter_step(DOWN, 3, t1)
        scatter_step(UP, 3, t2)
    diffuse_forward(-2)
    send_edges(forward[-1])
    for t in (c, d):
        scatter_step(DOWN, 2, t)
    diffuse_forward(2)
    send_edges(forward[1])
    for t in (c, d):
        scatter_step(UP, 2, t)
    for t in (a, b):
        scatter_step(DOWN, 2, t)
        scatter_step(UP, 2, t)
    diffuse_forward(-1)
    send_edges(forward[0])
    diffuse_forward(1)
    for t in (c, d, a, b):
        scatter_step(DOWN, 1, t)
        scatter_step(UP, 1, t)
    send_edges(observed)
    diffuse_forward(0)
    loads[4].wait()
    loads[5].wait()
    cross_step(c)
    cross_step(d)
    for copy in observed:
        copy.wait_recv()
    misfit_step(c)
    misfit_step(d)
    cross_step(a)
    cross_step(b)
    misfit_step(a)
    misfit_step(b)
    for k in range(1, 5):
        for t in (c, d, a, b):
            for way in (DOWN, UP):
                if k <= REACH[way][t]:
                    relay(way, k, t)
        if k == 1:
            adjoint(0)
            for off in (1, -1):
                adjoint(off)
            diffuse_backward(0)
        elif k < 4:
            for off in (k, -k):
                adjoint(off)
            for off in (k - 1, 1 - k):
                diffuse_backward(off)
        else:
            adjoint(4)
            for off in (3, -3, 4):
                diffuse_backward(off)

    for copy in sent:
        copy.wait_send()
    for copy in stored:
        copy.wait()


def body(alpha, perturb, kappa, land, obs_weight, innovation):
    f32, dma = jnp.float32, pltpu.SemaphoreType.DMA
    field = (OWN, PAIR, RING, ROWS, LON)
    slab = (SLOTS, PAIR, ROWS, LON)
    anywhere = pl.BlockSpec(memory_space=pl.ANY)
    grad, misfit = pl.pallas_call(
        kernel,
        out_shape=(
            jax.ShapeDtypeStruct(field, f32),
            jax.ShapeDtypeStruct((SLOTS, ROWS, LON), f32),
        ),
        in_specs=[anywhere] * 6,
        out_specs=(anywhere, anywhere),
        scratch_shapes=[
            pltpu.VMEM(field, f32),
            pltpu.VMEM((SLOTS,) + field, jnp.bfloat16),
            pltpu.VMEM(field, f32),
            pltpu.VMEM(field, f32),
            pltpu.VMEM(field, f32),
            pltpu.VMEM(field, f32),
            pltpu.VMEM((2 * ROWS, LON), f32),
            pltpu.VMEM((5, 2 * ROWS, LON), f32),
            pltpu.VMEM((ROWS, LON), jnp.int32),
            pltpu.VMEM((ROWS, LON), f32),
            pltpu.VMEM(field, f32),
            pltpu.VMEM((2, 5) + slab, f32),
            pltpu.VMEM(slab, f32),
            pltpu.VMEM(slab, f32),
            pltpu.VMEM((PAIR, 2, SLOTS, ROWS, LON), f32),
            pltpu.VMEM((RING,) + slab, f32),
            dma((6,)),
            dma((RING + SLOTS,)),
            dma((4,)),
            dma((RING, 2)),
            dma((RING, 2)),
            dma((RING, 2)),
            dma((RING, 2)),
            dma((2, 4, SLOTS)),
            dma((2, 4, SLOTS)),
            dma((SLOTS,)),
            dma((SLOTS,)),
            dma((2,)),
            dma((2,)),
            dma((2, 4, SLOTS)),
            dma((2, 4, SLOTS)),
        ],
        compiler_params=pltpu.CompilerParams(
            collective_id=0, has_side_effects=True, vmem_limit_bytes=40 * 2**20
        ),
    )(
        alpha.reshape(field),
        perturb.reshape((SLOTS,) + field),
        kappa,
        land,
        obs_weight.reshape(SLOTS, ROWS, LON),
        innovation.reshape(SLOTS, ROWS, LON),
    )
    return grad.reshape(alpha.shape), misfit.reshape(obs_weight.shape)


def solution(mesh):
    placed = (
        P("member", None, "space", None),
        P(None, "member", None, "space", None),
        P("space", None),
        P("space", None),
        P(None, "member", "space", None),
        P(None, "member", "space", None),
    )
    return jax.shard_map(
        body,
        mesh=mesh,
        in_specs=placed,
        out_specs=(P("member", None, "space", None), P(None, "member", "space", None)),
        check_vma=False,
    )
```

time: 469 us -> 93.5 us (0.20)
  the two profiles are of different devices: /device:TPU:8 before, /device:TPU:32 now
where the time goes in v1:
time: 93.5 us; the launch traced here: 91.9 us
  Pallas kernels  83.1 us (89%)
  local copies, waits for them, and re-layouts  8.16 us (9%)
    pallas_call x1, Pallas kernels, body(): pl.pallas_call(kernel, out_shape=(jax.ShapeDtypeStruct(field, f32), jax.S...  83.1 us
    unnamed x14, local copies, waits for them, and re-layouts  8.16 us

profile of v1, /device:TPU:32, one launch (start us, length us, event | category | flops | bytes accessed | tf_op | source)
XLA Modules:
  0.0 91.9 jit_solution(2641621065599622151)
XLA Ops:
  0.6 0.0 copy-start
  0.6 1.7 %copy-done = bf16[4,2,16,8,1280]{4,3,2,1,0:T(8,128)(2,1)S(1)} copy-done((bf16[4,2,16,8,1280]{4,3,2,1,0:T(8,128)(2,1)S(1)}, bf16[4,2,16,8,1280]{4,3,2,1,0:T(8,128)(2,1)}, u32[]{:S(2)}) %copy-start) | copy-done | bytes 2621464
  2.4 0.0 copy-start.1
  2.4 1.3 %copy-done.1 = f32[2,16,8,1280]{3,2,1,0:T(8,128)S(1)} copy-done((f32[2,16,8,1280]{3,2,1,0:T(8,128)S(1)}, f32[2,16,8,1280]{3,2,1,0:T(8,128)}, u32[]{:S(2)}) %copy-start.1) | copy-done | bytes 1310744
  3.7 0.0 copy-start.2
  3.7 0.9 copy-done.2
  4.6 0.0 copy-start.3
  4.6 0.9 copy-done.3
  5.5 0.0 copy-start.4
  5.5 0.8 copy-done.4
  6.3 0.0 copy-start.5
  6.3 0.8 copy-done.5
  7.1 83.1 %shard_map.77 = (f32[2,2,8,8,1280]{4,3,2,1,0:T(8,128)S(1)}, f32[4,8,1280]{2,1,0:T(8,128)S(1)}) custom-call(f32[2,2,8,8,1280]{4,3,2,1,0:T(8,128)S(1)} %bitcast.9, bf16[4,2,2,8,8,1280]{5,4,3,2,1,0:T(8,128)(2,1)S(1)} %bitcast.8, f32[8,1280]{1,0:T(8,128)S(1)} %copy-done.4, s32[8,1280]{1,0:T(8,128)S(1)} %copy-done.5, f32[4,8,1280]{2,1,0:T(8,128)S(1)} %bitcast.11, ...), custom_call_target="tpu_custom_call" | custom-call | tf_op jit(solution)/shard_map/pallas_call | solution.py:313
  90.2 1.1 %copy.11 = f32[2,16,8,1280]{3,2,1,0:T(8,128)} copy(f32[2,16,8,1280]{3,2,1,0:T(8,128)S(1)} %bitcast.10) | data formatting | bytes 2621440
  91.2 0.7 copy.12
Async XLA Ops:
  0.6 1.7 %copy-start = (bf16[4,2,16,8,1280]{4,3,2,1,0:T(8,128)(2,1)S(1)}, bf16[4,2,16,8,1280]{4,3,2,1,0:T(8,128)(2,1)}, u32[]{:S(2)}) copy-start(bf16[4,2,16,8,1280]{4,3,2,1,0:T(8,128)(2,1)} %param.7) | copy-start | bytes 7864324
  2.4 1.3 %copy-start.1 = (f32[2,16,8,1280]{3,2,1,0:T(8,128)S(1)}, f32[2,16,8,1280]{3,2,1,0:T(8,128)}, u32[]{:S(2)}) copy-start(f32[2,16,8,1280]{3,2,1,0:T(8,128)} %param.6) | copy-start | bytes 3932164
  3.7 0.9 copy-start.2
  4.6 0.9 copy-start.3
  5.5 0.8 copy-start.4
  6.3 0.8 copy-start.5

commit v2 on v1

--- a/solution.py
+++ b/solution.py
@@ -14,10 +14,32 @@
 SLOTS = 4
 OWN = 2
 SPACE = 16
+FIELDS = tuple((m, p) for m in range(OWN) for p in range(PAIR))
 MESH = pl.DeviceIdType.MESH
 DOWN, UP = 0, 1
 REACH = {DOWN: (4, 4, 3, 3), UP: (3, 3, 4, 4)}
 NEAR_LAST = (4, -3, 3, -2, 2, -1, 1, 0)
+
+ORDER = (
+    ("load", 1), ("forward", 4), ("edges", -2), ("load", 3), ("scatter", 0, 4, 0), ("scatter", 1, 4, 2),
+    ("scatter", 0, 4, 1), ("scatter", 1, 4, 3), ("forward", -3), ("edges", 2), ("scatter", 0, 3, 2),
+    ("scatter", 0, 3, 3), ("forward", 3), ("edges", -1), ("scatter", 1, 3, 0), ("forward", -2), ("edges", 1),
+    ("scatter", 1, 3, 2), ("scatter", 0, 3, 0), ("forward", 2), ("edges", 0), ("scatter", 1, 3, 3),
+    ("scatter", 1, 3, 1), ("observe",), ("forward", -1), ("scatter", 0, 2, 2), ("forward", 1), ("scatter", 0, 2, 3),
+    ("scatter", 1, 2, 2), ("scatter", 0, 3, 1), ("forward", 0), ("scatter", 1, 2, 3), ("scatter", 0, 2, 0),
+    ("scatter", 1, 2, 0), ("scatter", 0, 1, 2), ("scatter", 0, 1, 3), ("scatter", 1, 1, 2), ("scatter", 0, 2, 1),
+    ("scatter", 1, 1, 3), ("scatter", 1, 2, 1), ("scatter", 0, 1, 0), ("scatter", 1, 1, 0), ("observed",),
+    ("cross", 2), ("cross", 3), ("scatter", 0, 1, 1), ("scatter", 1, 1, 1), ("load", 5), ("load", 4), ("misfit", 2),
+    ("cross", 0), ("misfit", 3), ("cross", 1), ("relay", 0, 1, 2), ("relay", 1, 1, 2), ("misfit", 0),
+    ("relay", 0, 1, 3), ("relay", 1, 1, 3), ("misfit", 1), ("adjoint", 0), ("relay", 0, 2, 2), ("relay", 1, 2, 2),
+    ("relay", 0, 1, 0), ("relay", 1, 1, 0), ("backward", 0), ("relay", 0, 2, 3), ("relay", 1, 2, 3),
+    ("relay", 0, 1, 1), ("adjoint", 1), ("relay", 1, 1, 1), ("adjoint", -1), ("relay", 0, 3, 2), ("relay", 1, 3, 2),
+    ("relay", 0, 2, 0), ("relay", 1, 2, 0), ("backward", 1), ("relay", 0, 3, 3), ("relay", 1, 3, 3), ("backward", -1),
+    ("relay", 0, 2, 1), ("relay", 1, 2, 1), ("adjoint", -2), ("adjoint", 2), ("relay", 0, 3, 0), ("relay", 1, 4, 2),
+    ("relay", 1, 3, 0), ("relay", 0, 3, 1), ("adjoint", 3), ("backward", -2), ("relay", 0, 4, 0), ("relay", 1, 4, 3),
+    ("backward", 2), ("relay", 1, 3, 1), ("adjoint", -3), ("relay", 0, 4, 1), ("adjoint", 4), ("backward", 3),
+    ("backward", -3), ("backward", 4),
+)
 
 
 def kernel(
@@ -53,6 +75,9 @@
         copy.start()
         sent.append(copy)
 
+    barrier = pltpu.get_barrier_semaphore()
+    for device in (below, above, opposite, north, south):
+        pl.semaphore_signal(barrier, inc=1, device_id=device, device_id_type=MESH)
     loads = [
         pltpu.make_async_copy(kappa, kap.at[pl.ds(0, ROWS)], in_sem.at[0]),
         pltpu.make_async_copy(alpha, al, in_sem.at[1]),
@@ -64,9 +89,6 @@
     for load in loads:
         load.start()
 
-    barrier = pltpu.get_barrier_semaphore()
-    for device in (below, above, opposite, north, south):
-        pl.semaphore_signal(barrier, inc=1, device_id=device, device_id_type=MESH)
     pl.semaphore_wait(barrier, 5)
 
     low, high = pl.ds(0, HALO), pl.ds(HALO, HALO)
@@ -115,11 +137,11 @@
 
     send_edges(kap_copies)
     send_edges(forward[NEAR_LAST[0]])
-    send_edges(forward[NEAR_LAST[1]])
 
     loads[0].wait()
     for copy in kap_copies:
         copy.wait_recv()
+    send_edges(forward[NEAR_LAST[1]])
     row = lax.broadcasted_iota(jnp.int32, (2 * ROWS, LON), 0)
     inside = (row < ROWS) | ((row < ROWS + HALO) & (space < SPACE - 1)) | ((row >= ROWS + HALO) & (space > 0))
     k16 = jnp.where(inside, kap[...], 0.0)
@@ -129,6 +151,7 @@
     down = 0.5 * (k16 + pltpu.roll(k16, 1, 0))
     for i, c in enumerate((1.0 - (east + west + up + down), east, west, up, down)):
         coef[i] = jnp.where(inside, c, 0.0)
+    send_edges(forward[NEAR_LAST[2]])
     loads[2].wait()
     sea[...] = sea_i[...].astype(jnp.float32)
 
@@ -230,74 +253,21 @@
         copy.start()
         stored.append(copy)
 
-    a, b, c, d = range(SLOTS)
-    loads[1].wait()
-    diffuse_forward(4)
-    send_edges(forward[3])
-    loads[3].wait()
-    for way, t in ((DOWN, a), (UP, c), (DOWN, b), (UP, d)):
-        scatter_step(way, 4, t)
-    diffuse_forward(-3)
-    send_edges(forward[-2])
-    for t in (c, d):
-        scatter_step(DOWN, 3, t)
-    diffuse_forward(3)
-    send_edges(forward[2])
-    for t in (a, b):
-        scatter_step(UP, 3, t)
-    for t1, t2 in ((a, c), (b, d)):
-        scatter_step(DOWN, 3, t1)
-        scatter_step(UP, 3, t2)
-    diffuse_forward(-2)
-    send_edges(forward[-1])
-    for t in (c, d):
-        scatter_step(DOWN, 2, t)
-    diffuse_forward(2)
-    send_edges(forward[1])
-    for t in (c, d):
-        scatter_step(UP, 2, t)
-    for t in (a, b):
-        scatter_step(DOWN, 2, t)
-        scatter_step(UP, 2, t)
-    diffuse_forward(-1)
-    send_edges(forward[0])
-    diffuse_forward(1)
-    for t in (c, d, a, b):
-        scatter_step(DOWN, 1, t)
-        scatter_step(UP, 1, t)
-    send_edges(observed)
-    diffuse_forward(0)
-    loads[4].wait()
-    loads[5].wait()
-    cross_step(c)
-    cross_step(d)
-    for copy in observed:
-        copy.wait_recv()
-    misfit_step(c)
-    misfit_step(d)
-    cross_step(a)
-    cross_step(b)
-    misfit_step(a)
-    misfit_step(b)
-    for k in range(1, 5):
-        for t in (c, d, a, b):
-            for way in (DOWN, UP):
-                if k <= REACH[way][t]:
-                    relay(way, k, t)
-        if k == 1:
-            adjoint(0)
-            for off in (1, -1):
-                adjoint(off)
-            diffuse_backward(0)
-        elif k < 4:
-            for off in (k, -k):
-                adjoint(off)
-            for off in (k - 1, 1 - k):
-                diffuse_backward(off)
-        else:
-            adjoint(4)
-            for off in (3, -3, 4):
-                diffuse_backward(off)
+    tasks = {
+        "load": lambda i: loads[i].wait(),
+        "edges": lambda off: send_edges(forward[off]),
+        "forward": diffuse_forward,
+        "scatter": scatter_step,
+        "observe": lambda: send_edges(observed),
+        "observed": lambda: [copy.wait_recv() for copy in observed],
+        "cross": cross_step,
+        "misfit": misfit_step,
+        "relay": relay,
+        "adjoint": adjoint,
+        "backward": diffuse_backward,
+    }
+    for name, *details in ORDER:
+        tasks[name](*details)
 
     for copy in sent:
         copy.wait_send()
@@ -305,11 +275,25 @@
         copy.wait()
 
 
+def finish(grad, misfit, grad_out, misfit_out, held, held_misfit, in_sem, out_sem):
+    routes = [(misfit, held_misfit, misfit_out)]
+    routes += [(grad.at[m, p], held.at[m, p], grad_out.at[m, p]) for m, p in FIELDS]
+    arrive = [pltpu.make_async_copy(a, b, in_sem.at[i]) for i, (a, b, c) in enumerate(routes)]
+    leave = [pltpu.make_async_copy(b, c, out_sem.at[i]) for i, (a, b, c) in enumerate(routes)]
+    for copy in arrive:
+        copy.start()
+    for first, second in zip(arrive, leave):
+        first.wait()
+        second.start()
+    for copy in leave:
+        copy.wait()
+
+
 def body(alpha, perturb, kappa, land, obs_weight, innovation):
     f32, dma = jnp.float32, pltpu.SemaphoreType.DMA
     field = (OWN, PAIR, RING, ROWS, LON)
     slab = (SLOTS, PAIR, ROWS, LON)
-    anywhere = pl.BlockSpec(memory_space=pl.ANY)
+    anywhere = pl.BlockSpec(memory_space=pltpu.HBM)
     grad, misfit = pl.pallas_call(
         kernel,
         out_shape=(
@@ -352,7 +336,7 @@
             dma((2, 4, SLOTS)),
         ],
         compiler_params=pltpu.CompilerParams(
-            collective_id=0, has_side_effects=True, vmem_limit_bytes=40 * 2**20
+            collective_id=0, has_side_effects=True, vmem_limit_bytes=60 * 2**20
         ),
     )(
         alpha.reshape(field),
@@ -362,6 +346,22 @@
         obs_weight.reshape(SLOTS, ROWS, LON),
         innovation.reshape(SLOTS, ROWS, LON),
     )
+    grad, misfit = pl.pallas_call(
+        finish,
+        out_shape=(
+            jax.ShapeDtypeStruct(field, f32),
+            jax.ShapeDtypeStruct((SLOTS, ROWS, LON), f32),
+        ),
+        in_specs=[anywhere] * 2,
+        out_specs=(anywhere, anywhere),
+        scratch_shapes=[
+            pltpu.VMEM(field, f32),
+            pltpu.VMEM((SLOTS, ROWS, LON), f32),
+            dma((len(FIELDS) + 1,)),
+            dma((len(FIELDS) + 1,)),
+        ],
+        compiler_params=pltpu.CompilerParams(vmem_limit_bytes=60 * 2**20),
+    )(grad, misfit)
     return grad.reshape(alpha.shape), misfit.reshape(obs_weight.shape)
 
 

time: 93.5 us -> 82 us (0.88); the launches traced: 91.9 us -> 81.9 us
  local copies, waits for them, and re-layouts: 8.16 us -> 0 us
  Pallas kernels: 83.1 us -> 81.2 us
    unnamed x14 -> x0, local copies, waits for them, and re-layouts: 8.16 us -> none
    pallas_call x1, Pallas kernels: 83.1 us -> 79 us  [body(): pl.pallas_call(kernel, out_shape=(jax.ShapeDtypeStruct(field, f32), jax.S...]
    pallas_call x0 -> x1, Pallas kernels: none -> 2.19 us  [body(): pl.pallas_call(finish, out_shape=(jax.ShapeDtypeStruct(field, f32), jax.S...]
where the time goes in v2:
time: 82 us; the launch traced here: 81.9 us
  Pallas kernels  81.2 us (99%)
    pallas_call x1, Pallas kernels, body(): pl.pallas_call(kernel, out_shape=(jax.ShapeDtypeStruct(field, f32), jax.S...  79 us
    pallas_call x1, Pallas kernels, body(): pl.pallas_call(finish, out_shape=(jax.ShapeDtypeStruct(field, f32), jax.S...  2.19 us

profile of v2, /device:TPU:32, one launch (start us, length us, event | category | flops | bytes accessed | tf_op | source)
XLA Modules:
  0.0 81.9 jit_solution(7331881291940322965)
XLA Ops:
  0.6 79.0 %shard_map.77 = (f32[2,2,8,8,1280]{4,3,2,1,0:T(8,128)}, f32[4,8,1280]{2,1,0:T(8,128)}) custom-call(f32[2,2,8,8,1280]{4,3,2,1,0:T(8,128)} %bitcast.9, bf16[4,2,2,8,8,1280]{5,4,3,2,1,0:T(8,128)(2,1)} %bitcast.8, f32[8,1280]{1,0:T(8,128)} %kappa.1, s32[8,1280]{1,0:T(8,128)} %land.1, f32[4,8,1280]{2,1,0:T(8,128)} %bitcast.10, f32[4,8,1280]{2,1,0:T(8,128)} %bitcast.11), custom_call_target="tpu_custom_call" | custom-call | tf_op jit(solution)/shard_map/pallas_call | solution.py:297
  79.7 2.2 %shard_map.78 = (f32[2,2,8,8,1280]{4,3,2,1,0:T(8,128)}, f32[4,8,1280]{2,1,0:T(8,128)}) custom-call(f32[2,2,8,8,1280]{4,3,2,1,0:T(8,128)} %get-tuple-element.6.grad, f32[4,8,1280]{2,1,0:T(8,128)} %get-tuple-element.7.misfit), custom_call_target="tpu_custom_call" | custom-call | tf_op jit(solution)/shard_map/pallas_call | solution.py:349

commit v3 on v2

--- a/solution.py
+++ b/solution.py
@@ -14,6 +14,8 @@
 SLOTS = 4
 OWN = 2
 SPACE = 16
+LANES = 128
+FIRST = 4
 FIELDS = tuple((m, p) for m in range(OWN) for p in range(PAIR))
 MESH = pl.DeviceIdType.MESH
 DOWN, UP = 0, 1
@@ -23,11 +25,11 @@
 ORDER = (
     ("load", 1), ("forward", 4), ("edges", -2), ("load", 3), ("scatter", 0, 4, 0), ("scatter", 1, 4, 2),
     ("scatter", 0, 4, 1), ("scatter", 1, 4, 3), ("forward", -3), ("edges", 2), ("scatter", 0, 3, 2),
-    ("scatter", 0, 3, 3), ("forward", 3), ("edges", -1), ("scatter", 1, 3, 0), ("forward", -2), ("edges", 1),
-    ("scatter", 1, 3, 2), ("scatter", 0, 3, 0), ("forward", 2), ("edges", 0), ("scatter", 1, 3, 3),
-    ("scatter", 1, 3, 1), ("observe",), ("forward", -1), ("scatter", 0, 2, 2), ("forward", 1), ("scatter", 0, 2, 3),
-    ("scatter", 1, 2, 2), ("scatter", 0, 3, 1), ("forward", 0), ("scatter", 1, 2, 3), ("scatter", 0, 2, 0),
-    ("scatter", 1, 2, 0), ("scatter", 0, 1, 2), ("scatter", 0, 1, 3), ("scatter", 1, 1, 2), ("scatter", 0, 2, 1),
+    ("scatter", 0, 3, 3), ("forward", 3), ("edges", -1), ("scatter", 1, 3, 0), ("scatter", 0, 3, 0),
+    ("scatter", 1, 3, 2), ("forward", -2), ("edges", 1), ("scatter", 1, 3, 3), ("scatter", 1, 3, 1), ("forward", 2),
+    ("edges", 0), ("observe",), ("scatter", 0, 2, 2), ("forward", -1), ("scatter", 0, 2, 3), ("scatter", 1, 2, 2),
+    ("scatter", 0, 3, 1), ("forward", 1), ("scatter", 0, 2, 0), ("scatter", 1, 2, 3), ("scatter", 1, 2, 0),
+    ("forward", 0), ("scatter", 0, 1, 2), ("scatter", 0, 1, 3), ("scatter", 1, 1, 2), ("scatter", 0, 2, 1),
     ("scatter", 1, 1, 3), ("scatter", 1, 2, 1), ("scatter", 0, 1, 0), ("scatter", 1, 1, 0), ("observed",),
     ("cross", 2), ("cross", 3), ("scatter", 0, 1, 1), ("scatter", 1, 1, 1), ("load", 5), ("load", 4), ("misfit", 2),
     ("cross", 0), ("misfit", 3), ("cross", 1), ("relay", 0, 1, 2), ("relay", 1, 1, 2), ("misfit", 0),
@@ -35,9 +37,9 @@
     ("relay", 0, 1, 0), ("relay", 1, 1, 0), ("backward", 0), ("relay", 0, 2, 3), ("relay", 1, 2, 3),
     ("relay", 0, 1, 1), ("adjoint", 1), ("relay", 1, 1, 1), ("adjoint", -1), ("relay", 0, 3, 2), ("relay", 1, 3, 2),
     ("relay", 0, 2, 0), ("relay", 1, 2, 0), ("backward", 1), ("relay", 0, 3, 3), ("relay", 1, 3, 3), ("backward", -1),
-    ("relay", 0, 2, 1), ("relay", 1, 2, 1), ("adjoint", -2), ("adjoint", 2), ("relay", 0, 3, 0), ("relay", 1, 4, 2),
-    ("relay", 1, 3, 0), ("relay", 0, 3, 1), ("adjoint", 3), ("backward", -2), ("relay", 0, 4, 0), ("relay", 1, 4, 3),
-    ("backward", 2), ("relay", 1, 3, 1), ("adjoint", -3), ("relay", 0, 4, 1), ("adjoint", 4), ("backward", 3),
+    ("relay", 0, 2, 1), ("adjoint", 2), ("relay", 1, 2, 1), ("adjoint", -2), ("relay", 0, 3, 0), ("relay", 1, 4, 2),
+    ("relay", 1, 3, 0), ("relay", 0, 3, 1), ("adjoint", 3), ("backward", 2), ("relay", 1, 4, 3), ("relay", 0, 4, 0),
+    ("backward", -2), ("relay", 1, 3, 1), ("adjoint", -3), ("relay", 0, 4, 1), ("adjoint", 4), ("backward", 3),
     ("backward", -3), ("backward", 4),
 )
 
@@ -45,7 +47,7 @@
 def kernel(
     alpha, perturb, kappa, land, weight, innov,
     grad_out, misfit_out,
-    al, pe, halo_f, halo_b, back, result, kap, coef, sea_i, sea,
+    al, pe, halo_f, halo_b, back, result, work, kap, coef, coef_own, sea_i, sea,
     local, ring, total, across, obs, misfit,
     in_sem, out_sem, kap_sem, hf_send, hf_recv, hb_send, hb_recv,
     rs_send, rs_recv, x_send, x_recv, ob_send, ob_recv, ag_send, ag_recv,
@@ -79,7 +81,7 @@
     for device in (below, above, opposite, north, south):
         pl.semaphore_signal(barrier, inc=1, device_id=device, device_id_type=MESH)
     loads = [
-        pltpu.make_async_copy(kappa, kap.at[pl.ds(0, ROWS)], in_sem.at[0]),
+        pltpu.make_async_copy(kappa, kap.at[pl.ds(HALO, ROWS)], in_sem.at[0]),
         pltpu.make_async_copy(alpha, al, in_sem.at[1]),
         pltpu.make_async_copy(land, sea_i, in_sem.at[2]),
         pltpu.make_async_copy(perturb, pe, in_sem.at[3]),
@@ -89,12 +91,13 @@
     for load in loads:
         load.start()
 
+    work[...] = jnp.zeros_like(work)
     pl.semaphore_wait(barrier, 5)
 
     low, high = pl.ds(0, HALO), pl.ds(HALO, HALO)
     kap_copies = (
-        remote(kappa.at[high], kap.at[pl.ds(ROWS + HALO, HALO)], kap_sem.at[0], kap_sem.at[1], north),
-        remote(kappa.at[low], kap.at[pl.ds(ROWS, HALO)], kap_sem.at[2], kap_sem.at[3], south),
+        remote(kappa.at[high], kap.at[pl.ds(0, HALO)], kap_sem.at[0], kap_sem.at[1], north),
+        remote(kappa.at[low], kap.at[pl.ds(HALO + ROWS, HALO)], kap_sem.at[2], kap_sem.at[3], south),
     )
 
     def edges(src, dst, send, recv, off):
@@ -143,46 +146,69 @@
         copy.wait_recv()
     send_edges(forward[NEAR_LAST[1]])
     row = lax.broadcasted_iota(jnp.int32, (2 * ROWS, LON), 0)
-    inside = (row < ROWS) | ((row < ROWS + HALO) & (space < SPACE - 1)) | ((row >= ROWS + HALO) & (space > 0))
+    row8 = lax.broadcasted_iota(jnp.int32, (LON // LANES, ROWS, LANES), 1)
+    known = ((row8 < HALO) & (space < SPACE - 1)) | ((row8 >= HALO) & (space > 0))
+
+    def apart(x):
+        return jnp.stack([x[:, n * LANES : (n + 1) * LANES] for n in range(LON // LANES)])
+
+    inside = ((row >= HALO) | (space > 0)) & ((row < HALO + ROWS) | (space < SPACE - 1))
     k16 = jnp.where(inside, kap[...], 0.0)
     east = 0.5 * (k16 + pltpu.roll(k16, LON - 1, 1))
     west = 0.5 * (k16 + pltpu.roll(k16, 1, 1))
     up = 0.5 * (k16 + pltpu.roll(k16, 2 * ROWS - 1, 0))
     down = 0.5 * (k16 + pltpu.roll(k16, 1, 0))
     for i, c in enumerate((1.0 - (east + west + up + down), east, west, up, down)):
-        coef[i] = jnp.where(inside, c, 0.0)
+        c = jnp.where(inside, c, 0.0)
+        coef[i] = apart(c)
+        coef_own[i] = apart(c[HALO : HALO + ROWS])
     send_edges(forward[NEAR_LAST[2]])
     loads[2].wait()
     sea[...] = sea_i[...].astype(jnp.float32)
 
-    def smooth(tile, edge):
-        row8 = lax.broadcasted_iota(jnp.int32, (ROWS, LON), 0)
-        known = ((row8 < HALO) & (space < SPACE - 1)) | ((row8 >= HALO) & (space > 0))
-        u = jnp.concatenate([tile, jnp.where(known, edge, 0.0)], axis=0)
+    count = LON // LANES
+    lane = lax.broadcasted_iota(jnp.int32, (count, ROWS, LANES), 2)
+
+    def smooth(tiles, edges, store):
+        for f, (tile, edge) in enumerate(zip(tiles, edges)):
+            work[0, f, :, FIRST + HALO : FIRST + HALO + ROWS] = apart(tile)
+            edge = jnp.where(known, apart(edge), 0.0)
+            work[0, f, :, FIRST : FIRST + HALO] = edge[:, HALO:]
+            work[0, f, :, FIRST + HALO + ROWS : FIRST + 2 * ROWS] = edge[:, :HALO]
         for step in range(STEPS):
-            n = 2 * ROWS if step < STEPS - 1 else ROWS
-            terms = (
-                u,
-                pltpu.roll(u, LON - 1, 1),
-                pltpu.roll(u, 1, 1),
-                pltpu.roll(u, 2 * ROWS - 1, 0),
-                pltpu.roll(u, 1, 0),
-            )
-            acc = coef[0, :n] * terms[0][:n]
-            for i in range(1, 5):
-                acc = acc + coef[i, :n] * terms[i][:n]
-            u = acc
-        return u
+            now, later = step % 2, 1 - step % 2
+            last = step == STEPS - 1
+            starts = (FIRST + HALO,) if last else (FIRST, FIRST + ROWS)
+            table = coef_own if last else coef
+            for f in range(len(tiles)):
+                for i, start in enumerate(starts):
+                    u = work[now, f, :, pl.ds(start, ROWS)]
+                    ahead = jnp.concatenate([u[1:], u[:1]], axis=0)
+                    behind = jnp.concatenate([u[-1:], u[:-1]], axis=0)
+                    terms = (
+                        u,
+                        pltpu.roll(jnp.where(lane == 0, ahead, u), LANES - 1, 2),
+                        pltpu.roll(jnp.where(lane == LANES - 1, behind, u), 1, 2),
+                        work[now, f, :, pl.ds(start + 1, ROWS)],
+                        work[now, f, :, pl.ds(start - 1, ROWS)],
+                    )
+                    t = [table[q, :, pl.ds(i * ROWS, ROWS)] * term for q, term in enumerate(terms)]
+                    value = ((t[0] + t[1]) + (t[2] + t[3])) + t[4]
+                    if last:
+                        store(f, jnp.concatenate([value[n] for n in range(count)], axis=1))
+                    else:
+                        work[later, f, :, pl.ds(start, ROWS)] = value
 
     def diffuse_forward(off):
         for copy in forward[off]:
             copy.wait_recv()
         z = at(off)
 
-        @pl.loop(0, OWN * PAIR)
-        def _(i):
-            m, p = i // PAIR, lax.rem(i, PAIR)
-            local[m, p, z] = smooth(al[m, p, z], halo_f[m, p, z]) * sea[...]
+        def store(f, value):
+            m, p = FIELDS[f]
+            local[m, p, z] = value * sea[...]
+
+        smooth([al[m, p, z] for m, p in FIELDS], [halo_f[m, p, z] for m, p in FIELDS], store)
 
     def partial(off, t, p):
         z = at(off)
@@ -244,10 +270,11 @@
             copy.wait_recv()
         z = at(off)
 
-        @pl.loop(0, OWN * PAIR)
-        def _(i):
-            m, p = i // PAIR, lax.rem(i, PAIR)
-            result[m, p, z] = smooth(back[m, p, z], halo_b[m, p, z]) + al[m, p, z]
+        def store(f, value):
+            m, p = FIELDS[f]
+            result[m, p, z] = value + al[m, p, z]
+
+        smooth([back[m, p, z] for m, p in FIELDS], [halo_b[m, p, z] for m, p in FIELDS], store)
 
         copy = pltpu.make_async_copy(result.at[:, :, z], grad_out.at[:, :, z], out_sem.at[off % RING])
         copy.start()
@@ -309,8 +336,10 @@
             pltpu.VMEM(field, f32),
             pltpu.VMEM(field, f32),
             pltpu.VMEM(field, f32),
+            pltpu.VMEM((2, OWN * PAIR, LON // LANES, 3 * ROWS, LANES), f32),
             pltpu.VMEM((2 * ROWS, LON), f32),
-            pltpu.VMEM((5, 2 * ROWS, LON), f32),
+            pltpu.VMEM((5, LON // LANES, 2 * ROWS, LANES), f32),
+            pltpu.VMEM((5, LON // LANES, ROWS, LANES), f32),
             pltpu.VMEM((ROWS, LON), jnp.int32),
             pltpu.VMEM((ROWS, LON), f32),
             pltpu.VMEM(field, f32),

time: 82 us -> 78 us (0.951)
  Pallas kernels: 81.2 us -> 77.1 us
    pallas_call x1, Pallas kernels: 79 us -> 74.9 us  [body(): pl.pallas_call(kernel, out_shape=(jax.ShapeDtypeStruct(field, f32), jax.S...]
where the time goes in v3:
time: 78 us; the launch traced here: 77.9 us
  Pallas kernels  77.1 us (99%)
  between operations  0.8 us (1%)
    pallas_call x1, Pallas kernels, body(): pl.pallas_call(kernel, out_shape=(jax.ShapeDtypeStruct(field, f32), jax.S...  74.9 us
    pallas_call x1, Pallas kernels, body(): pl.pallas_call(finish, out_shape=(jax.ShapeDtypeStruct(field, f32), jax.S...  2.19 us

profile of v3, /device:TPU:32, one launch (start us, length us, event | category | flops | bytes accessed | tf_op | source)
XLA Modules:
  0.0 77.9 jit_solution(6544451899504350410)
XLA Ops:
  0.6 74.9 %shard_map.77 = (f32[2,2,8,8,1280]{4,3,2,1,0:T(8,128)}, f32[4,8,1280]{2,1,0:T(8,128)}) custom-call(f32[2,2,8,8,1280]{4,3,2,1,0:T(8,128)} %bitcast.9, bf16[4,2,2,8,8,1280]{5,4,3,2,1,0:T(8,128)(2,1)} %bitcast.8, f32[8,1280]{1,0:T(8,128)} %kappa.1, s32[8,1280]{1,0:T(8,128)} %land.1, f32[4,8,1280]{2,1,0:T(8,128)} %bitcast.10, f32[4,8,1280]{2,1,0:T(8,128)} %bitcast.11), custom_call_target="tpu_custom_call" | custom-call | tf_op jit(solution)/shard_map/pallas_call | solution.py:324
  75.5 2.2 %shard_map.78 = (f32[2,2,8,8,1280]{4,3,2,1,0:T(8,128)}, f32[4,8,1280]{2,1,0:T(8,128)}) custom-call(f32[2,2,8,8,1280]{4,3,2,1,0:T(8,128)} %get-tuple-element.6.grad, f32[4,8,1280]{2,1,0:T(8,128)} %get-tuple-element.7.misfit), custom_call_target="tpu_custom_call" | custom-call | tf_op jit(solution)/shard_map/pallas_call | solution.py:378
